TPU v7x, 256 devices: a whole 4x4x8 slice. The times are simulated.
256 devices in a mesh: replica: 32 (over z_hi, x, core), fsdp: 8 (over z_lo, y).
Axes of the slice: x: 4, y: 4, z: 8 (z_hi: 4, z_lo: 2; z = z_hi * 2 + z_lo), core: 2. Of those that a mesh axis runs over, the one named last changes fastest.
Arguments:
- layer_input: bfloat16 [32, 2, 1024, 12288], P('replica', None, 'fsdp'), may hold values from -6 to 6
- cotangent: bfloat16 [32, 2, 1024, 256], P('replica', None, 'fsdp'), may hold values from -6 to 6
- weight: bfloat16 [32, 12288, 256], P('replica', 'fsdp'), may hold values from -5 to 5
- first_moment: float32 [32, 12288, 256], P('replica', 'fsdp'), may hold values from -0.2 to 0.2
- second_moment: float32 [32, 12288, 256], P('replica', 'fsdp'), may hold values from 0.01 to 0.1
- key_gain: float32 [128], replicated, may hold values from 0.5 to 1.5
- frag_index: int32 [1], replicated, may hold values from 0 to 4095
- anchor: float32 [12288, 128], P('fsdp'), may hold values from -5 to 5
- momentum: float32 [12288, 128], P('fsdp'), may hold values from -3 to 3
Outputs:
- merged_weight: bfloat16 [32, 12288, 256], P('replica', 'fsdp')
- new_momentum: float32 [12288, 128], P('fsdp')
- new_anchor: float32 [12288, 128], P('fsdp')
Inputs may be any that keep to these rules, and one draw needn't show every extreme that they name: `frag_index`: the same plan position for all replicas.
All inputs are finite; a program needn't handle non-finite values.
Results may differ from a plain program's by a relative error of at most 0.014.
Values may be sent and summed in bfloat16 or wider, within the bound.
A program may use at most 128 MiB of HBM per device.

v0:
```python
import math

import jax
import jax.numpy as jnp
from jax import lax
from jax.sharding import PartitionSpec as P

D = 12288
HEAD = 128
KV = 2
TOK_DEV = 128
STEPS = 2


beta_first = 0.9
beta_second = 0.95
inner_rate = 2.0
decay_rate = 0.05
adam_eps = 1e-08
norm_eps = 1e-06
outer_rate = 0.7
outer_beta = 0.9
mix_local = 0.5


def norm_backward(keys_raw, upstream, key_gain):
    tokens_count, columns = keys_raw.shape
    grouped = keys_raw.reshape(tokens_count, columns // HEAD, HEAD)
    scaled_up = upstream.astype(jnp.float32).reshape(tokens_count, columns // HEAD, HEAD) * key_gain
    inverse = lax.rsqrt(jnp.mean(grouped * grouped, axis=-1, keepdims=True) + norm_eps)
    inner_prod = jnp.mean(scaled_up * grouped, axis=-1, keepdims=True)
    result = inverse * scaled_up - grouped * (inverse * inverse * inverse) * inner_prod
    return result.reshape(tokens_count, columns).astype(jnp.bfloat16)


def adamw(weight_now, moment_one, moment_two, gradient):
    moment_one = beta_first * moment_one + (1.0 - beta_first) * gradient
    moment_two = beta_second * moment_two + (1.0 - beta_second) * gradient * gradient
    master = weight_now.astype(jnp.float32)
    master = master - inner_rate * (
        moment_one / (jnp.sqrt(moment_two) + adam_eps) + decay_rate * master
    )
    return (master.astype(jnp.bfloat16), moment_one, moment_two)


def outer_update(delta_mean, anchor_part, momentum_part):
    momentum_next = outer_beta * momentum_part + delta_mean
    anchor_next = anchor_part - outer_rate * (delta_mean + outer_beta * momentum_next)
    return (momentum_next, anchor_next)


def body(
    layer_input,
    cotangent,
    weight,
    first_moment,
    second_moment,
    key_gain,
    frag_index,
    anchor,
    momentum,
):
    groups = lax.axis_size("fsdp")
    replicas = lax.axis_size("replica")
    tokens_all = layer_input[0]
    upstream_all = cotangent[0]
    weight_now = weight[0]
    moment_one = first_moment[0]
    moment_two = second_moment[0]
    width_scale = 1.0 / math.sqrt(D)
    token_scale = 1.0 / math.sqrt(TOK_DEV * groups)
    first_col = frag_index[0] % KV * HEAD
    fragment = lax.dynamic_slice_in_dim(weight_now, first_col, HEAD, 1).astype(jnp.float32)
    pseudo = anchor - fragment
    summed = lax.psum(pseudo, "replica")
    new_momentum, new_anchor = outer_update(summed / replicas, anchor, momentum)
    for inner_step in range(STEPS):
        tokens_now = tokens_all[inner_step]
        keys_raw = (
            jnp.dot(
                tokens_now,
                lax.all_gather(weight_now, "fsdp", axis=0, tiled=True),
                preferred_element_type=jnp.float32,
            )
            * width_scale
        )
        delta_keys = norm_backward(keys_raw, upstream_all[inner_step], key_gain)
        gradient = (
            lax.psum_scatter(
                lax.dot_general(
                    tokens_now,
                    delta_keys,
                    (((0,), (0,)), ((), ())),
                    preferred_element_type=jnp.float32,
                ).astype(jnp.bfloat16),
                "fsdp",
                scatter_dimension=0,
                tiled=True,
            ).astype(jnp.float32)
            * token_scale
        )
        weight_now, moment_one, moment_two = adamw(weight_now, moment_one, moment_two, gradient)
    local_frag = lax.dynamic_slice_in_dim(weight_now, first_col, HEAD, 1).astype(jnp.float32)
    mixed_cols = (mix_local * local_frag + (1.0 - mix_local) * new_anchor).astype(jnp.bfloat16)
    merged = lax.dynamic_update_slice_in_dim(weight_now, mixed_cols, first_col, 1)
    return (merged[None], new_momentum, new_anchor)


def solution(mesh):
    placed = (
        P("replica", None, "fsdp", None),
        P("replica", None, "fsdp", None),
        P("replica", "fsdp", None),
        P("replica", "fsdp", None),
        P("replica", "fsdp", None),
        P(),
        P(),
        P("fsdp", None),
        P("fsdp", None),
    )
    return jax.shard_map(
        body,
        mesh=mesh,
        in_specs=placed,
        out_specs=(P("replica", "fsdp", None), P("fsdp", None), P("fsdp", None)),
        check_vma=False,
    )
```

profile of v0, /device:TPU:2, one launch (start us, length us, event | category | flops | bytes accessed | tf_op | source)
XLA Modules:
  0.0 540.2 jit_solution(3299268429000732167)
XLA Ops:
  8.8 0.9 slice_convert_fusion
  10.4 78.1 %all-gather.6.cloned.1.call-done = bf16[1,12288,256]{2,1,0:T(8,128)(2,1)} async-done(((bf16[1,1536,256]{2,1,0:T(8,128)(2,1)}), bf16[1,12288,256]{2,1,0:T(8,128)(2,1)}) %all-gather.6.cloned.1.call-update) | async-done | bytes 6291472 | tf_op jit(solution)/shard_map/all_gather | solution.py:82
  88.5 4.7 fusion.34
  94.6 6.4 %fusion = bf16[12288,256]{0,1:T(8,128)(2,1)} fusion(bf16[1,2,128,12288]{3,2,1,0:T(8,128)(2,1)} %param.9, f32[16,8,2,128]{3,2,1,0:T(2,128)S(1)} %bitcast.119, f32[128,256]{1,0:T(8,128)S(1)} %fusion.34, f32[16,8,2,128]{3,2,1,0:T(2,128)S(1)} %bitcast.121, f32[16,8,2,128]{3,2,1,0:T(2,128)S(1)} %bitcast.123, f32[256]{0:T(256)S(1)} %broadcast_bitcast_fusion, ...), kind=kOutput, calls=%fused_computation.2 | convolution fusion | flops 808681472 | bytes 10028032 | tf_op jit(solution)/shard_map/dot_general | solution.py:90
  101.1 1.0 copy-done.2
  102.2 1.2 copy.40
  103.8 1.9 copy.47
  105.7 69.8 %reduce-scatter.3.cloned.1.call-done = bf16[1536,256]{0,1:T(8,128)(2,1)} async-done(((bf16[12288,256]{0,1:T(8,128)(2,1)}), bf16[1536,256]{0,1:T(8,128)(2,1)}) %reduce-scatter.3.cloned.1.call-update) | async-done | bytes 786448 | tf_op jit(solution)/shard_map/reduce_scatter | solution.py:89
  175.4 3.5 fusion.18
  179.7 2.3 copy.57
  182.0 2.3 convert_subtract_fusion.2
  184.6 68.2 %all-gather.4.cloned.1.call-done = bf16[12288,256]{0,1:T(8,128)(2,1)} async-done(((bf16[1536,256]{0,1:T(8,128)(2,1)}), bf16[12288,256]{0,1:T(8,128)(2,1)}) %all-gather.4.cloned.1.call-update) | async-done | bytes 6291472 | tf_op jit(solution)/shard_map/all_gather | solution.py:82
  252.8 5.9 %fusion.31 = f32[128,256]{1,0:T(8,128)S(1)} fusion(bf16[12288,256]{0,1:T(8,128)(2,1)} %all-gather.4.cloned.1.call-done, bf16[1,2,128,12288]{3,2,1,0:T(8,128)(2,1)} %param.9), kind=kOutput, calls=%fused_computation.41 | convolution fusion | flops 805339136 | bytes 9568256 | tf_op jit(solution)/shard_map/dot_general | solution.py:80
  259.4 1.9 multiply_reduce_fusion.1
  261.4 0.9 copy.49
  264.0 6.4 %fusion.1 = bf16[12288,256]{0,1:T(8,128)(2,1)} fusion(bf16[1,2,128,12288]{3,2,1,0:T(8,128)(2,1)} %param.9, f32[16,8,2,128]{3,2,1,0:T(2,128)S(1)} %bitcast.118, f32[128,256]{1,0:T(8,128)S(1)} %fusion.31, f32[16,8,2,128]{3,2,1,0:T(2,128)S(1)} %bitcast.120, f32[16,8,2,128]{3,2,1,0:T(2,128)S(1)} %bitcast.122, f32[256]{0:T(256)S(1)} %broadcast_bitcast_fusion, ...), kind=kOutput, calls=%fused_computation.3 | convolution fusion | flops 808681472 | bytes 10028032 | tf_op jit(solution)/shard_map/dot_general | solution.py:90
  270.4 2.4 copy.56
  272.8 247.5 %all-reduce.2.cloned.1.call-done = f32[1536,128]{0,1:T(8,128)} async-done(((f32[1536,128]{0,1:T(8,128)}), f32[1536,128]{0,1:T(8,128)}) %all-reduce.2.cloned.1.call-update) | async-done | bytes 786448 | tf_op jit(solution)/shard_map/psum | solution.py:75
  520.2 2.4 multiply_add_fusion
  522.7 2.3 copy.59
  525.0 4.1 fusion.15
  529.2 1.0 copy-done
  530.8 1.2 copy.58
  531.9 1.1 copy.60
  (47 shorter events, 6.8 us)
Async XLA Ops:
  8.0 80.5 %all-gather.6.cloned.1.call-start = ((), (), s32[]{:S(2)}) async-start(), calls=%async_computation.6 | async-start | bytes 7077888 | tf_op jit(solution)/shard_map/all_gather | solution.py:82
  8.7 166.7 %reduce-scatter.3.cloned.1.call-start = ((), (), s32[]{:S(2)}) async-start(), calls=%async_computation.2 | async-start | bytes 7077888 | tf_op jit(solution)/shard_map/reduce_scatter | solution.py:89
  10.4 82.9 %copy-start.6 = (f32[128]{0:T(128)S(1)}, f32[128]{0:T(128)}, u32[]{:S(2)}) copy-start(f32[128]{0:T(128)} %param.14) | copy-start | bytes 1540
  93.2 1.4 copy-start.5
  101.0 1.1 copy-start.2
  101.0 2.3 copy-start.4
  101.1 151.7 %all-gather.4.cloned.1.call-start = ((), (), s32[]{:S(2)}) async-start(), calls=%async_computation.3 | async-start | bytes 7077888 | tf_op jit(solution)/shard_map/all_gather | solution.py:82
  179.0 341.3 %all-reduce.2.cloned.1.call-start = ((), (), s32[]{:S(2)}) async-start(), calls=%async_computation.5 | async-start | bytes 1572864 | tf_op jit(solution)/shard_map/psum | solution.py:75
  184.3 340.7 %reduce-scatter.5.cloned.1.call-start = ((), (), s32[]{:S(2)}) async-start(), calls=%async_computation.4 | async-start | bytes 7077888 | tf_op jit(solution)/shard_map/reduce_scatter | solution.py:89
  525.0 4.2 copy-start.3
  529.1 1.1 copy-start
  529.1 1.4 copy-start.1
Sparse Core Ops, SparseCore 0:
  10.6 77.8 all-gather.5
  101.2 74.2 reduce-scatter.2
  179.1 73.6 all-gather.3
  270.5 74.7 reduce-scatter.4
Sparse Core Ops, SparseCore 1:
  184.3 335.8 all-reduce.1
where the time goes:
time: 547 us; the launch traced here: 540 us
  waiting for transfers between devices  464 us (85%)
  matrix products  23.4 us (4%)
  local copies, waits for them, and re-layouts  19.4 us (4%)
  other arithmetic  16.7 us (3%)
  between operations  16.1 us (3%)
    psum x1, waiting for transfers between devices, body(): summed = lax.psum(pseudo, 'replica')  247 us
    all_gather x2, waiting for transfers between devices, body(): lax.all_gather(weight_now, 'fsdp', axis=0, tiled=True)  146 us
    reduce_scatter x2, waiting for transfers between devices, body(): lax.psum_scatter(lax.dot_general(tokens_now, delta_keys, (((0,), (0,)), (...  69.8 us
    unnamed x23, local copies, waits for them, and re-layouts  15.1 us
    dot_general x2, matrix products, body(): lax.dot_general(tokens_now, delta_keys, (((0,), (0,)), ((), ())), preferr...  12.8 us
  transfers between devices with their start and end apart: 5, of which 4 were waited for; matrix products, arithmetic and copies ran while one was open for 6% of the time, Pallas kernels for 0%

commit v1 on v0

v1 whole, which is shorter than its diff:
```python
import math

import jax
import jax.numpy as jnp
from jax import lax
from jax.experimental import pallas as pl
from jax.experimental.pallas import tpu as pltpu
from jax.sharding import PartitionSpec as P

D = 12288
HEAD = 128
KV = 2
C = KV * HEAD
TOK = 128
STEPS = 2
FSDP = 8
ROWS = D // FSDP
REPLICAS = 32
SPLITS = (2, 4)
TILE = 256

beta_first = 0.9
beta_second = 0.95
inner_rate = 2.0
decay_rate = 0.05
adam_eps = 1e-08
norm_eps = 1e-06
outer_rate = 0.7
outer_beta = 0.9
mix_local = 0.5

PLANE = ((1, 2), (0, 2), (1, 1), (1, 3), (0, 1), (0, 3), (1, 0))
LAYER = tuple((dx, dc) for dx in (2, 1, 3, 0) for dc in (0, 1) if (dx, dc) != (0, 0))
LAYERS = (2, 1, 3)
SEG = ROWS // 8
PIECE = SEG // 4
MESH = pl.DeviceIdType.MESH


def kernel(
    x_hbm, cot_hbm, w_hbm, m_hbm, v_hbm, gain_ref, frag_ref, anchor_hbm, mom_hbm,
    merged_hbm, newmom_hbm, newanchor_hbm,
    xbuf0, xbuf1, rsend0, rsend1, rrecv0, rrecv1, dbuf0, dbuf1,
    cot, w_now, m_now, v_now, grad, anchor, mom, out_w,
    frag, layer_in, partial, pieces, total,
    loc_sem, xs0, xr0, xs1, xr1, rs, rr, ds, dr, ls, lr, ps, pr, qs, qr, ts, tr, own_sem,
):
    rep = lax.axis_index("replica")
    fs = lax.axis_index("fsdp")
    zl, yy = fs // 4, lax.rem(fs, 4)
    zh, xx, cc = rep // 8, lax.rem(rep // 2, 4), lax.rem(rep, 2)

    def plane_index(dz, dy):
        return lax.rem(zl + dz, 2) * 4 + lax.rem(yy + dy, 4)

    def layer_index(dx, dc):
        return lax.rem(xx + dx, 4) * 2 + lax.rem(cc + dc, 2)

    def plane_dev(dz, dy):
        return (rep, plane_index(dz, dy))

    def layer_dev(dx, dc):
        return (zh * 8 + layer_index(dx, dc), fs)

    def stack_dev(dh):
        return (lax.rem(zh + dh, 4) * 8 + xx * 2 + cc, fs)

    partners = (
        [plane_dev(*o) for o in PLANE] + [layer_dev(*o) for o in LAYER] + [stack_dev(h) for h in LAYERS]
    )
    with jax.named_scope("entry"):
        bar = pltpu.get_barrier_semaphore()
        for p in partners:
            pl.semaphore_signal(bar, inc=1, device_id=p, device_id_type=MESH)
        pl.semaphore_wait(bar, len(partners))

    sends = []

    def remote(src, dst, s, r, dev):
        cp = pltpu.make_async_remote_copy(
            src_ref=src, dst_ref=dst, send_sem=s, recv_sem=r, device_id=dev, device_id_type=MESH
        )
        cp.start()
        sends.append(cp)
        return cp

    def slot(dz, dy):
        return dz * 4 + dy

    def back(dz, dy):
        return dz * 4 + (4 - dy) % 4

    xbufs, xss, xrs = (xbuf0, xbuf1), (xs0, xs1), (xr0, xr1)
    rsends, rrecvs, dbufs = (rsend0, rsend1), (rrecv0, rrecv1), (dbuf0, dbuf1)
    first_unit = (0, SPLITS[0])

    def columns(dz, dy):
        return pl.ds(pl.multiple_of(plane_index(dz, dy) * ROWS, 128), ROWS)

    def send_x(step, h):
        n = TOK // SPLITS[step]
        got = []
        for i, o in enumerate(PLANE):
            got.append(
                remote(
                    x_hbm.at[0, step, pl.ds(h * n, n), columns(*o)],
                    xbufs[step].at[h, pl.ds(back(*o) * n, n)],
                    xss[step].at[h, i],
                    xrs[step].at[h, i],
                    plane_dev(*o),
                )
            )
        own = pltpu.make_async_copy(
            x_hbm.at[0, step, pl.ds(h * n, n), columns(0, 0)],
            xbufs[step].at[h, pl.ds(0, n)],
            own_sem.at[first_unit[step] + h],
        )
        own.start()
        return got, own

    def local(src, dst, i):
        cp = pltpu.make_async_copy(src, dst, loc_sem.at[i])
        cp.start()
        return cp

    xcp = {}
    with jax.named_scope("send_x"):
        for h in range(SPLITS[0]):
            xcp[0, h] = send_x(0, h)
        get_w = local(w_hbm.at[0], w_now, 0)
        get_cot = local(cot_hbm.at[0], cot, 1)
        get_m = local(m_hbm.at[0], m_now, 2)
        get_v = local(v_hbm.at[0], v_now, 3)
        get_anchor = local(anchor_hbm, anchor, 4)
        get_mom = local(mom_hbm, mom, 5)
        for h in range(SPLITS[1]):
            xcp[1, h] = send_x(1, h)

    first_frag = lax.rem(frag_ref[0], KV) == 0
    lane_first = jnp.where(first_frag, jnp.float32(1.0), jnp.float32(0.0))

    def segment(dx, dc):
        return pl.ds(pl.multiple_of(layer_index(dx, dc) * SEG, 16), SEG)

    with jax.named_scope("fragment"):
        get_w.wait()
        frag[...] = jnp.where(
            lane_first > 0.5, w_now[:, :HEAD].astype(jnp.float32), w_now[:, HEAD:].astype(jnp.float32)
        ).astype(jnp.bfloat16)
        layer_cps = []
        for i, (dx, dc) in enumerate(LAYER):
            layer_cps.append(
                remote(frag.at[segment(dx, dc)], layer_in.at[i], ls.at[i], lr.at[i], layer_dev(dx, dc))
            )

    width_scale = 1.0 / math.sqrt(D)
    token_scale = 1.0 / math.sqrt(TOK * FSDP)
    unit = lambda step, h: first_unit[step] + h
    rcp, dcp = {}, {}

    def stage_raw(step, h):
        n = TOK // SPLITS[step]
        got, own = xcp[step, h]
        with jax.named_scope(f"wait_x_{step}_{h}"):
            own.wait()
            for cp in got:
                cp.wait_recv()
        with jax.named_scope(f"raw_{step}_{h}"):
            rsends[step][h] = jnp.dot(
                xbufs[step][h], w_now[...], preferred_element_type=jnp.float32
            ).astype(jnp.bfloat16)
            cps = []
            for i, o in enumerate(PLANE):
                cps.append(
                    remote(
                        rsends[step].at[h, pl.ds(slot(*o) * n, n)],
                        rrecvs[step].at[h, i],
                        rs.at[unit(step, h), i],
                        rr.at[unit(step, h), i],
                        plane_dev(*o),
                    )
                )
            rcp[step, h] = cps

    def stage_delta(step, h):
        n = TOK // SPLITS[step]
        with jax.named_scope(f"wait_raw_{step}_{h}"):
            for cp in rcp[step, h]:
                cp.wait_recv()
        with jax.named_scope(f"delta_{step}_{h}"):
            raw = rsends[step][h, :n].astype(jnp.float32)
            for i in range(len(PLANE)):
                raw = raw + rrecvs[step][h, i].astype(jnp.float32)
            raw = raw * width_scale
            up = cot[step, pl.ds(h * n, n)].astype(jnp.float32)
            gain = gain_ref[...]
            for k in range(KV):
                cols = slice(k * HEAD, (k + 1) * HEAD)
                g = raw[:, cols]
                p = up[:, cols] * gain
                inv = lax.rsqrt(jnp.mean(g * g, axis=-1, keepdims=True) + norm_eps)
                dotp = jnp.mean(p * g, axis=-1, keepdims=True)
                dbufs[step][h, :n, cols] = (inv * p - g * (inv * inv * inv) * dotp).astype(jnp.bfloat16)
            cps = []
            for i, o in enumerate(PLANE):
                cps.append(
                    remote(
                        dbufs[step].at[h, pl.ds(0, n)],
                        dbufs[step].at[h, pl.ds(back(*o) * n, n)],
                        ds.at[unit(step, h), i],
                        dr.at[unit(step, h), i],
                        plane_dev(*o),
                    )
                )
            dcp[step, h] = cps

    def stage_grad(step, h, finish):
        with jax.named_scope(f"wait_delta_{step}_{h}"):
            for cp in dcp[step, h]:
                cp.wait_recv()
        with jax.named_scope(f"grad_{step}_{h}"):
            d = dbufs[step][h]
            for t in range(ROWS // TILE):
                rows = pl.ds(t * TILE, TILE)
                g = lax.dot_general(
                    xbufs[step][h, :, rows], d, (((0,), (0,)), ((), ())), preferred_element_type=jnp.float32
                )
                if h > 0:
                    g = g + grad[rows]
                if finish is None:
                    grad[rows] = g
                else:
                    finish(rows, g * token_scale)

    def adamw(rows, g):
        m = beta_first * m_now[rows] + (1.0 - beta_first) * g
        v = beta_second * v_now[rows] + (1.0 - beta_second) * g * g
        w = w_now[rows].astype(jnp.float32)
        w = w - inner_rate * (m / (jnp.sqrt(v) + adam_eps) + decay_rate * w)
        return w.astype(jnp.bfloat16), m, v

    def finish_first(rows, g):
        w, m, v = adamw(rows, g)
        w_now[rows] = w
        m_now[rows] = m
        v_now[rows] = v

    def finish_last(rows, g):
        w, _, _ = adamw(rows, g)
        mixed = anchor[rows]
        for k in range(KV):
            cols = slice(k * HEAD, (k + 1) * HEAD)
            mine = w[:, cols].astype(jnp.float32)
            chosen = lane_first > 0.5 if k == 0 else lane_first < 0.5
            out_w[rows, cols] = jnp.where(
                chosen, mix_local * mine + (1.0 - mix_local) * mixed, mine
            ).astype(jnp.bfloat16)

    def layer_sum():
        with jax.named_scope("layer_sum"):
            for cp in layer_cps:
                cp.wait_recv()
            s = frag[segment(0, 0)].astype(jnp.float32)
            for i in range(len(LAYER)):
                s = s + layer_in[i].astype(jnp.float32)
            partial[...] = s
            cps = []
            for i, dh in enumerate(LAYERS):
                where = pl.ds(pl.multiple_of(lax.rem(zh + dh, 4) * PIECE, 8), PIECE)
                cps.append(remote(partial.at[where], pieces.at[i], ps.at[i], pr.at[i], stack_dev(dh)))
            return cps

    def stack_sum(cps):
        with jax.named_scope("stack_sum"):
            for cp in cps:
                cp.wait_recv()
            s = partial[pl.ds(pl.multiple_of(zh * PIECE, 8), PIECE)]
            for i in range(len(LAYERS)):
                s = s + pieces[i]
            mine = pl.ds(pl.multiple_of(layer_index(0, 0) * SEG + zh * PIECE, 8), PIECE)
            total[mine] = s
            out = []
            for i, dh in enumerate(LAYERS):
                out.append(remote(total.at[mine], total.at[mine], qs.at[i], qr.at[i], stack_dev(dh)))
            return out

    def layer_gather(cps):
        with jax.named_scope("layer_gather"):
            for cp in cps:
                cp.wait_recv()
            out = []
            for i, (dx, dc) in enumerate(LAYER):
                out.append(
                    remote(
                        total.at[segment(0, 0)], total.at[segment(0, 0)], ts.at[i], tr.at[i], layer_dev(dx, dc)
                    )
                )
            return out

    def outer(cps):
        with jax.named_scope("outer"):
            for cp in cps:
                cp.wait_recv()
            get_anchor.wait()
            get_mom.wait()
            a = anchor[...]
            mean = a - total[...] * (1.0 / REPLICAS)
            nm = outer_beta * mom[...] + mean
            mom[...] = nm
            anchor[...] = a - outer_rate * (mean + outer_beta * nm)
            return [local(mom, newmom_hbm, 4), local(anchor, newanchor_hbm, 5)]

    stage_raw(0, 0)
    get_cot.wait()
    stage_delta(0, 0)
    layer_out = layer_sum()
    stage_raw(0, 1)
    stage_delta(0, 1)
    get_m.wait()
    get_v.wait()
    stage_grad(0, 0, None)
    stack_out = stack_sum(layer_out)
    stage_grad(0, 1, finish_first)
    gather_out = layer_gather(stack_out)
    last = SPLITS[1] - 1
    stage_raw(1, 0)
    stage_delta(1, 0)
    outs = outer(gather_out)
    for h in range(1, last + 1):
        stage_raw(1, h)
        stage_grad(1, h - 1, None)
        stage_delta(1, h)
    stage_grad(1, last, finish_last)
    with jax.named_scope("write"):
        put = local(out_w, merged_hbm.at[0], 0)
        for cp in sends:
            cp.wait_send()
        for cp in outs:
            cp.wait()
        put.wait()


def body(layer_input, cotangent, weight, first_moment, second_moment, key_gain, frag_index, anchor, momentum):
    bf, f32 = jnp.bfloat16, jnp.float32
    units = sum(SPLITS)
    dma = pltpu.SemaphoreType.DMA
    any_spec = pl.BlockSpec(memory_space=pl.ANY)
    scratch = [
        pltpu.VMEM((SPLITS[0], TOK * FSDP // SPLITS[0], ROWS), bf),
        pltpu.VMEM((SPLITS[1], TOK * FSDP // SPLITS[1], ROWS), bf),
        pltpu.VMEM((SPLITS[0], TOK * FSDP // SPLITS[0], C), bf),
        pltpu.VMEM((SPLITS[1], TOK * FSDP // SPLITS[1], C), bf),
        pltpu.VMEM((SPLITS[0], 7, TOK // SPLITS[0], C), bf),
        pltpu.VMEM((SPLITS[1], 7, TOK // SPLITS[1], C), bf),
        pltpu.VMEM((SPLITS[0], TOK * FSDP // SPLITS[0], C), bf),
        pltpu.VMEM((SPLITS[1], TOK * FSDP // SPLITS[1], C), bf),
        pltpu.VMEM((STEPS, TOK, C), bf),
        pltpu.VMEM((ROWS, C), bf),
        pltpu.VMEM((ROWS, C), f32),
        pltpu.VMEM((ROWS, C), f32),
        pltpu.VMEM((ROWS, C), f32),
        pltpu.VMEM((ROWS, HEAD), f32),
        pltpu.VMEM((ROWS, HEAD), f32),
        pltpu.VMEM((ROWS, C), bf),
        pltpu.VMEM((ROWS, HEAD), bf),
        pltpu.VMEM((len(LAYER), SEG, HEAD), bf),
        pltpu.VMEM((SEG, HEAD), f32),
        pltpu.VMEM((len(LAYERS), PIECE, HEAD), f32),
        pltpu.VMEM((ROWS, HEAD), f32),
        dma((6,)),
        dma((SPLITS[0], 7)),
        dma((SPLITS[0], 7)),
        dma((SPLITS[1], 7)),
        dma((SPLITS[1], 7)),
        dma((units, 7)),
        dma((units, 7)),
        dma((units, 7)),
        dma((units, 7)),
        dma((7,)),
        dma((7,)),
        dma((3,)),
        dma((3,)),
        dma((3,)),
        dma((3,)),
        dma((7,)),
        dma((7,)),
        dma((units,)),
    ]
    return pl.pallas_call(
        kernel,
        name="inner_outer",
        out_shape=(
            jax.ShapeDtypeStruct((1, ROWS, C), bf),
            jax.ShapeDtypeStruct((ROWS, HEAD), f32),
            jax.ShapeDtypeStruct((ROWS, HEAD), f32),
        ),
        in_specs=[any_spec] * 5
        + [pl.BlockSpec(memory_space=pltpu.VMEM), pl.BlockSpec(memory_space=pltpu.SMEM)]
        + [any_spec] * 2,
        out_specs=(any_spec, any_spec, any_spec),
        scratch_shapes=scratch,
        compiler_params=pltpu.CompilerParams(
            collective_id=0, has_side_effects=True, vmem_limit_bytes=62 << 20
        ),
    )(
        layer_input, cotangent, weight, first_moment, second_moment,
        key_gain.reshape(1, HEAD), frag_index, anchor, momentum,
    )


def solution(mesh):
    placed = (
        P("replica", None, "fsdp", None),
        P("replica", None, "fsdp", None),
        P("replica", "fsdp", None),
        P("replica", "fsdp", None),
        P("replica", "fsdp", None),
        P(),
        P(),
        P("fsdp", None),
        P("fsdp", None),
    )
    return jax.shard_map(
        body,
        mesh=mesh,
        in_specs=placed,
        out_specs=(P("replica", "fsdp", None), P("fsdp", None), P("fsdp", None)),
        check_vma=False,
    )
```

time: 547 us -> 137 us (0.25); the launches traced: 540 us -> 137 us
  waiting for transfers between devices: 464 us -> 0 us
  Pallas kernels: 0 us -> 132 us
  matrix products: 23.4 us -> 0 us
  other arithmetic: 16.7 us -> 0 us
  local copies, waits for them, and re-layouts: 19.4 us -> 3.95 us
  between operations: 16.1 us -> 1.3 us
    psum x1 -> x0, waiting for transfers between devices: 247 us -> none  [body(): summed = lax.psum(pseudo, 'replica')]
    all_gather x2 -> x0, waiting for transfers between devices: 146 us -> none  [body(): lax.all_gather(weight_now, 'fsdp', axis=0, tiled=True)]
    pallas_call x0 -> x1, Pallas kernels: none -> 132 us  [body(): pl.pallas_call(kernel, name='inner_outer', out_shape=(jax.ShapeDtypeStruc...]
    reduce_scatter x2 -> x0, waiting for transfers between devices: 69.8 us -> none  [body(): lax.psum_scatter(lax.dot_general(tokens_now, delta_keys, (((0,), (0,)), (...]
    dot_general x4 -> x0, matrix products: 23.4 us -> none  [the longest x2 12.8 us: body(): lax.dot_general(tokens_now, delta_keys, (((0,), (0,)), ((), ())), preferr...]
    unnamed x23 -> x7, local copies, waits for them, and re-layouts: 15.1 us -> 3.95 us
    convert_element_type x3 -> x0, other arithmetic: 8.49 us -> none  [the longest x2 7.6 us: adamw(): return (master.astype(jnp.bfloat16), moment_one, moment_two)]
  transfers between devices with their start and end apart: 5 -> 0, of which waited for: 4 -> 0; matrix products, arithmetic and copies ran while one was open for 6% -> 0% of each run, Pallas kernels for 0% -> 0%
where the time goes in v1:
time: 137 us
  Pallas kernels  132 us (96%)
  local copies, waits for them, and re-layouts  3.95 us (3%)
    pallas_call x1, Pallas kernels, body(): pl.pallas_call(kernel, name='inner_outer', out_shape=(jax.ShapeDtypeStruc...  132 us
    unnamed x7, local copies, waits for them, and re-layouts  3.95 us

profile of v1, /device:TPU:2, one launch (start us, length us, event | category | flops | bytes accessed | tf_op | source)
XLA Modules:
  0.0 137.0 jit_solution(416805340565060116)
XLA Ops:
  1.3 131.8 %inner_outer.1 = (bf16[1,1536,256]{2,1,0:T(8,128)(2,1)}, f32[1536,128]{1,0:T(8,128)}, f32[1536,128]{1,0:T(8,128)}) custom-call(bf16[1,2,128,12288]{3,2,1,0:T(8,128)(2,1)} %x_hbm.1, bf16[1,2,128,256]{3,2,1,0:T(8,128)(2,1)} %cot_hbm.1, bf16[1,1536,256]{2,1,0:T(8,128)(2,1)} %w_hbm.1, f32[1,1536,256]{2,1,0:T(8,128)} %m_hbm.1, f32[1,1536,256]{2,1,0:T(8,128)} %v_hbm.1, ...), custom_call_target="tpu_custom_call" | custom-call | tf_op jit(solution)/shard_map/inner_outer/pallas_call | solution.py:389
  133.1 0.0 copy-start.1
  133.1 0.0 copy-start
  133.1 2.2 %copy.16 = bf16[1,1536,256]{2,1,0:T(8,128)(2,1)} copy(bf16[1,1536,256]{2,1,0:T(8,128)(2,1)} %get-tuple-element.6) | data formatting | bytes 1572864
  135.3 0.0 copy-done.1
  135.3 0.9 copy.17
  136.1 0.0 copy-done
  136.1 0.9 copy.18
Async XLA Ops:
  133.1 2.2 %copy-start.1 = (f32[1536,128]{1,0:T(8,128)S(1)}, f32[1536,128]{1,0:T(8,128)}, u32[]{:S(2)}) copy-start(f32[1536,128]{1,0:T(8,128)} %get-tuple-element.7) | copy-start | bytes 2359300
  133.1 3.1 %copy-start = (f32[1536,128]{1,0:T(8,128)S(1)}, f32[1536,128]{1,0:T(8,128)}, u32[]{:S(2)}) copy-start(f32[1536,128]{1,0:T(8,128)} %get-tuple-element.8) | copy-start | bytes 2359300

commit v2 on v1

v2 whole, which is shorter than its diff:
```python
import math

import jax
import jax.numpy as jnp
from jax import lax
from jax.experimental import pallas as pl
from jax.experimental.pallas import tpu as pltpu
from jax.sharding import PartitionSpec as P

D = 12288
HEAD = 128
KV = 2
C = KV * HEAD
TOK = 128
STEPS = 2
FSDP = 8
ROWS = D // FSDP
REPLICAS = 32
GROUPS = ((64, 64), (64, 48, 16))
SIZES = ((32, 32, 32, 32), (32, 32, 32, 16, 16))
AHEAD = 64
UNITS = tuple((s, sum(SIZES[s][:i]), n) for s in range(STEPS) for i, n in enumerate(SIZES[s]))
EXCH = tuple((s, g) for s in range(STEPS) for g in range(len(GROUPS[s])))
TILE = 256
PARTS = 2
LIMIT = 61 << 20

beta_first = 0.9
beta_second = 0.95
inner_rate = 2.0
decay_rate = 0.05
adam_eps = 1e-08
norm_eps = 1e-06
outer_rate = 0.7
outer_beta = 0.9
mix_local = 0.5

PLANE = ((1, 2), (0, 2), (1, 1), (1, 3), (0, 1), (0, 3), (1, 0))
LAYER = tuple((dx, dc) for dx in (2, 1, 3, 0) for dc in (0, 1) if (dx, dc) != (0, 0))
LAYERS = (2, 1, 3)
SEG = ROWS // 8
PIECE = SEG // 4
MESH = pl.DeviceIdType.MESH


def kernel(
    x_hbm, cot_hbm, w_hbm, m_hbm, v_hbm, gain_ref, frag_ref, anchor_hbm, mom_hbm,
    out_w, newmom, newanchor,
    *scratch,
):
    count = len(EXCH)
    xbufs = dict(zip(EXCH, scratch[:count]))
    rsends = dict(zip(EXCH, scratch[count : 2 * count]))
    rrecvs = dict(zip(EXCH, scratch[2 * count : 3 * count]))
    dbufs = dict(zip(EXCH, scratch[3 * count : 4 * count]))
    (
        cot, w_now, m_now, v_now, grad, anchor, mom, frag, layer_in, partial, pieces, total,
        loc_sem, own_sem, xs, xr, rs, rr, ds, dr, ls, lr, ps, pr, qs, qr, ts, tr, go_sem,
    ) = scratch[4 * count :]
    rep = lax.axis_index("replica")
    fs = lax.axis_index("fsdp")
    zl, yy = fs // 4, lax.rem(fs, 4)
    zh, xx, cc = rep // 8, lax.rem(rep // 2, 4), lax.rem(rep, 2)

    def plane_index(dz, dy):
        return lax.rem(zl + dz, 2) * 4 + lax.rem(yy + dy, 4)

    def layer_index(dx, dc):
        return lax.rem(xx + dx, 4) * 2 + lax.rem(cc + dc, 2)

    def plane_dev(dz, dy):
        return (rep, plane_index(dz, dy))

    def layer_dev(dx, dc):
        return (zh * 8 + layer_index(dx, dc), fs)

    def stack_dev(dh):
        return (lax.rem(zh + dh, 4) * 8 + xx * 2 + cc, fs)

    leader = rep == REPLICAS - 1
    with jax.named_scope("entry"):
        bar = pltpu.get_barrier_semaphore()
        for o in PLANE:
            pl.semaphore_signal(bar, inc=1, device_id=plane_dev(*o), device_id_type=MESH)

        @pl.when(jnp.logical_not(leader))
        def _():
            pl.semaphore_signal(bar, inc=1, device_id=(REPLICAS - 1, fs), device_id_type=MESH)
            pl.semaphore_wait(bar, len(PLANE))

        @pl.when(leader)
        def _():
            pl.semaphore_wait(bar, len(PLANE) + REPLICAS - 1)

    sends = []

    def remote(src, dst, s, r, dev):
        cp = pltpu.make_async_remote_copy(
            src_ref=src, dst_ref=dst, send_sem=s, recv_sem=r, device_id=dev, device_id_type=MESH
        )
        cp.start()
        sends.append(cp)
        return cp

    def arrive(cps, name):
        for cp in cps:
            cp.wait_recv()

    def slot(dz, dy):
        return dz * 4 + dy

    def back(dz, dy):
        return dz * 4 + (4 - dy) % 4

    def columns(dz, dy):
        return pl.ds(pl.multiple_of(plane_index(dz, dy) * ROWS, 128), ROWS)

    def place(step, row):
        g = 0
        while row >= GROUPS[step][g]:
            row -= GROUPS[step][g]
            g += 1
        return g, row

    def send_x(k):
        step, row, rows = UNITS[k]
        g, at = place(step, row)
        n = GROUPS[step][g]
        got = []
        for i, o in enumerate(PLANE):
            got.append(
                remote(
                    x_hbm.at[0, step, pl.ds(row, rows), columns(*o)],
                    xbufs[step, g].at[pl.ds(back(*o) * n + at, rows)],
                    xs.at[k, i],
                    xr.at[k, i],
                    plane_dev(*o),
                )
            )
        own = pltpu.make_async_copy(
            x_hbm.at[0, step, pl.ds(row, rows), columns(0, 0)],
            xbufs[step, g].at[pl.ds(at, rows)],
            own_sem.at[k],
        )
        own.start()
        return got, own

    def local(src, dst, i):
        cp = pltpu.make_async_copy(src, dst, loc_sem.at[i])
        cp.start()
        return cp

    xcp = {}

    def issue(k):
        if k < len(UNITS):
            with jax.named_scope("send_x"):
                xcp[k] = send_x(k)

    def landed(k):
        with jax.named_scope("wait_x"):
            got, own = xcp[k]
            own.wait()
            arrive(got, f"x_{k}")

    issued = 0
    done = 0
    position = 0

    def top_up():
        nonlocal issued, done
        while issued < len(UNITS) and (issued == 0 or sum(u[2] for u in UNITS[:issued]) < position + AHEAD):
            issue(issued)
            issued += 1

    top_up()
    get_w = local(w_hbm.at[0], w_now, 0)
    get_cot = local(cot_hbm.at[0], cot, 1)
    get_m = local(m_hbm.at[0], m_now, 2)
    get_v = local(v_hbm.at[0], v_now, 3)
    get_anchor = local(anchor_hbm, anchor, 4)
    get_mom = local(mom_hbm, mom, 5)

    first_frag = lax.rem(frag_ref[0], KV) == 0
    lane_first = jnp.where(first_frag, jnp.float32(1.0), jnp.float32(0.0))

    def segment(dx, dc):
        return pl.ds(pl.multiple_of(layer_index(dx, dc) * SEG, 16), SEG)

    def open_layers():
        with jax.named_scope("open_layers"):

            @pl.when(leader)
            def _():
                @pl.loop(0, REPLICAS - 1)
                def _(r):
                    pl.semaphore_signal(go_sem, inc=1, device_id=(r, fs), device_id_type=MESH)

            get_w.wait()
            frag[...] = jnp.where(
                lane_first > 0.5, w_now[:, :HEAD].astype(jnp.float32), w_now[:, HEAD:].astype(jnp.float32)
            ).astype(jnp.bfloat16)

    def layer_scatter():
        with jax.named_scope("layer_scatter"):

            @pl.when(jnp.logical_not(leader))
            def _():
                pl.semaphore_wait(go_sem, 1)

            return [
                remote(frag.at[segment(dx, dc)], layer_in.at[i], ls.at[i], lr.at[i], layer_dev(dx, dc))
                for i, (dx, dc) in enumerate(LAYER)
            ]

    width_scale = 1.0 / math.sqrt(D)
    token_scale = 1.0 / math.sqrt(TOK * FSDP)
    rcp, dcp = {}, {}

    def stage_raw(step, g):
        n = GROUPS[step][g]
        e = EXCH.index((step, g))
        with jax.named_scope(f"raw_{step}_{g}"):
            rsends[step, g][...] = jnp.dot(
                xbufs[step, g][...], w_now[...], preferred_element_type=jnp.float32
            ).astype(jnp.bfloat16)
            cps = []
            for i, o in enumerate(PLANE):
                cps.append(
                    remote(
                        rsends[step, g].at[pl.ds(slot(*o) * n, n)],
                        rrecvs[step, g].at[i],
                        rs.at[e, i],
                        rr.at[e, i],
                        plane_dev(*o),
                    )
                )
            rcp[step, g] = cps

    def stage_delta(step, g):
        n = GROUPS[step][g]
        e = EXCH.index((step, g))
        with jax.named_scope(f"wait_raw_{step}_{g}"):
            arrive(rcp[step, g], f"raw_{step}_{g}")
        with jax.named_scope(f"delta_{step}_{g}"):
            raw = rsends[step, g][:n].astype(jnp.float32)
            for i in range(len(PLANE)):
                raw = raw + rrecvs[step, g][i].astype(jnp.float32)
            raw = raw * width_scale
            up = cot[step, pl.ds(sum(GROUPS[step][:g]), n)].astype(jnp.float32)
            gain = gain_ref[...]
            for k in range(KV):
                cols = slice(k * HEAD, (k + 1) * HEAD)
                r = raw[:, cols]
                p = up[:, cols] * gain
                inv = lax.rsqrt(jnp.mean(r * r, axis=-1, keepdims=True) + norm_eps)
                dotp = jnp.mean(p * r, axis=-1, keepdims=True)
                dbufs[step, g][:n, cols] = (inv * p - r * (inv * inv * inv) * dotp).astype(jnp.bfloat16)
            cps = []
            for i, o in enumerate(PLANE):
                cps.append(
                    remote(
                        dbufs[step, g].at[pl.ds(0, n)],
                        dbufs[step, g].at[pl.ds(back(*o) * n, n)],
                        ds.at[e, i],
                        dr.at[e, i],
                        plane_dev(*o),
                    )
                )
            dcp[step, g] = cps

    def stage_grad(step, g, finish):
        with jax.named_scope(f"wait_delta_{step}_{g}"):
            arrive(dcp[step, g], f"delta_{step}_{g}")
        with jax.named_scope(f"grad_{step}_{g}"):
            d = dbufs[step, g][...]
            for t in range(ROWS // TILE):
                rows = pl.ds(t * TILE, TILE)
                acc = lax.dot_general(
                    xbufs[step, g][:, rows], d, (((0,), (0,)), ((), ())), preferred_element_type=jnp.float32
                )
                if g > 0:
                    acc = acc + grad[rows]
                if finish is None:
                    grad[rows] = acc
                else:
                    finish(rows, acc * token_scale)

    def adamw(rows, g):
        m = beta_first * m_now[rows] + (1.0 - beta_first) * g
        v = beta_second * v_now[rows] + (1.0 - beta_second) * g * g
        w = w_now[rows].astype(jnp.float32)
        w = w - inner_rate * (m / (jnp.sqrt(v) + adam_eps) + decay_rate * w)
        return w.astype(jnp.bfloat16), m, v

    def finish_first(rows, g):
        w, m, v = adamw(rows, g)
        w_now[rows] = w
        m_now[rows] = m
        v_now[rows] = v

    def finish_last(rows, g):
        w, _, _ = adamw(rows, g)
        mixed = newanchor[rows]
        for k in range(KV):
            cols = slice(k * HEAD, (k + 1) * HEAD)
            mine = w[:, cols].astype(jnp.float32)
            chosen = lane_first > 0.5 if k == 0 else lane_first < 0.5
            out_w[0, rows, cols] = jnp.where(
                chosen, mix_local * mine + (1.0 - mix_local) * mixed, mine
            ).astype(jnp.bfloat16)

    def layer_sum(layer_cps):
        with jax.named_scope("layer_sum"):
            arrive(layer_cps, "layer")
            s = frag[segment(0, 0)].astype(jnp.float32)
            for i in range(len(LAYER)):
                s = s + layer_in[i].astype(jnp.float32)
            partial[...] = s
            cps = []
            for i, dh in enumerate(LAYERS):
                where = pl.ds(pl.multiple_of(lax.rem(zh + dh, 4) * PIECE, 8), PIECE)
                cps.append(remote(partial.at[where], pieces.at[i], ps.at[i], pr.at[i], stack_dev(dh)))
            return cps

    def stack_sum(cps):
        with jax.named_scope("stack_sum"):
            arrive(cps, "stack_sum")
            s = partial[pl.ds(pl.multiple_of(zh * PIECE, 8), PIECE)]
            for i in range(len(LAYERS)):
                s = s + pieces[i]
            mine = pl.ds(pl.multiple_of(layer_index(0, 0) * SEG + zh * PIECE, 8), PIECE)
            total[mine] = s
            out = []
            for i, dh in enumerate(LAYERS):
                out.append(remote(total.at[mine], total.at[mine], qs.at[i], qr.at[i], stack_dev(dh)))
            return out

    def layer_gather(cps):
        with jax.named_scope("layer_gather"):
            arrive(cps, "layer_gather")
            out = []
            for i, (dx, dc) in enumerate(LAYER):
                out.append(
                    remote(
                        total.at[segment(0, 0)], total.at[segment(0, 0)], ts.at[i], tr.at[i], layer_dev(dx, dc)
                    )
                )
            return out

    def outer(cps):
        with jax.named_scope("outer"):
            arrive(cps, "outer")
            get_anchor.wait()
            get_mom.wait()
            a = anchor[...]
            mean = a - total[...] * (1.0 / REPLICAS)
            nm = outer_beta * mom[...] + mean
            newmom[...] = nm
            newanchor[...] = a - outer_rate * (mean + outer_beta * nm)

    held = {}

    def first_moments():
        get_m.wait()
        get_v.wait()

    def hold(name, value):
        held[name] = value

    todo = {
        48: [lambda: hold("scatter", layer_scatter())],
        64: [lambda: get_cot.wait(), lambda: stage_raw(0, 0)],
        96: [lambda: stage_delta(0, 0)],
        112: [lambda: hold("layer", layer_sum(held["scatter"]))],
        128: [lambda: stage_raw(0, 1), lambda: stage_grad(0, 0, None)],
        144: [lambda: hold("stack", stack_sum(held["layer"]))],
        160: [lambda: stage_delta(0, 1)],
        176: [lambda: hold("gather", layer_gather(held["stack"]))],
        192: [first_moments, lambda: stage_grad(0, 1, finish_first), lambda: stage_raw(1, 0)],
        208: [lambda: outer(held["gather"])],
        224: [lambda: stage_delta(1, 0)],
        240: [lambda: stage_raw(1, 1)],
        256: [
            lambda: stage_raw(1, 2),
            lambda: stage_grad(1, 0, None),
            lambda: stage_delta(1, 1),
            lambda: stage_delta(1, 2),
            lambda: stage_grad(1, 1, None),
            lambda: stage_grad(1, 2, finish_last),
        ],
    }
    open_layers()
    for k in range(len(UNITS)):
        landed(k)
        before = position
        position += UNITS[k][2]
        for mark in sorted(todo):
            if before < mark <= position:
                for act in todo[mark]:
                    act()
        top_up()
    with jax.named_scope("write"):
        for cp in sends:
            cp.wait_send()


def flush(a_ref, b_ref, c_ref, a_out, b_out, c_out, sems):
    cps = []
    n = ROWS // PARTS
    for k in range(PARTS):
        part = pl.ds(k * n, n)
        cps.append(pltpu.make_async_copy(a_ref.at[0, part], a_out.at[0, part], sems.at[0, k]))
        cps.append(pltpu.make_async_copy(b_ref.at[part], b_out.at[part], sems.at[1, k]))
        cps.append(pltpu.make_async_copy(c_ref.at[part], c_out.at[part], sems.at[2, k]))
    for cp in cps:
        cp.start()
    for cp in cps:
        cp.wait()


def body(layer_input, cotangent, weight, first_moment, second_moment, key_gain, frag_index, anchor, momentum):
    bf, f32 = jnp.bfloat16, jnp.float32
    dma = pltpu.SemaphoreType.DMA
    any_spec = pl.BlockSpec(memory_space=pltpu.HBM)
    sizes = [GROUPS[s][g] for s, g in EXCH]
    scratch = [pltpu.VMEM((FSDP * n, ROWS), bf) for n in sizes]
    scratch += [pltpu.VMEM((FSDP * n, C), bf) for n in sizes]
    scratch += [pltpu.VMEM((len(PLANE), n, C), bf) for n in sizes]
    scratch += [pltpu.VMEM((FSDP * n, C), bf) for n in sizes]
    scratch += [
        pltpu.VMEM((STEPS, TOK, C), bf),
        pltpu.VMEM((ROWS, C), bf),
        pltpu.VMEM((ROWS, C), f32),
        pltpu.VMEM((ROWS, C), f32),
        pltpu.VMEM((ROWS, C), f32),
        pltpu.VMEM((ROWS, HEAD), f32),
        pltpu.VMEM((ROWS, HEAD), f32),
        pltpu.VMEM((ROWS, HEAD), bf),
        pltpu.VMEM((len(LAYER), SEG, HEAD), bf),
        pltpu.VMEM((SEG, HEAD), f32),
        pltpu.VMEM((len(LAYERS), PIECE, HEAD), f32),
        pltpu.VMEM((ROWS, HEAD), f32),
        dma((6,)),
        dma((len(UNITS),)),
        dma((len(UNITS), 7)),
        dma((len(UNITS), 7)),
        dma((len(EXCH), 7)),
        dma((len(EXCH), 7)),
        dma((len(EXCH), 7)),
        dma((len(EXCH), 7)),
        dma((7,)),
        dma((7,)),
        dma((3,)),
        dma((3,)),
        dma((3,)),
        dma((3,)),
        dma((7,)),
        dma((7,)),
        pltpu.SemaphoreType.REGULAR,
    ]
    vmem_spec = pl.BlockSpec(memory_space=pltpu.VMEM)
    outs = pl.pallas_call(
        kernel,
        name="inner_outer",
        out_shape=(
            pltpu.VMEM((1, ROWS, C), bf),
            pltpu.VMEM((ROWS, HEAD), f32),
            pltpu.VMEM((ROWS, HEAD), f32),
        ),
        in_specs=[any_spec] * 5 + [vmem_spec, pl.BlockSpec(memory_space=pltpu.SMEM)] + [any_spec] * 2,
        out_specs=(vmem_spec, vmem_spec, vmem_spec),
        scratch_shapes=scratch,
        compiler_params=pltpu.CompilerParams(
            collective_id=0, has_side_effects=True, vmem_limit_bytes=LIMIT
        ),
    )(
        layer_input, cotangent, weight, first_moment, second_moment,
        key_gain.reshape(1, HEAD), frag_index, anchor, momentum,
    )
    return outs


def solution(mesh):
    placed = (
        P("replica", None, "fsdp", None),
        P("replica", None, "fsdp", None),
        P("replica", "fsdp", None),
        P("replica", "fsdp", None),
        P("replica", "fsdp", None),
        P(),
        P(),
        P("fsdp", None),
        P("fsdp", None),
    )
    return jax.shard_map(
        body,
        mesh=mesh,
        in_specs=placed,
        out_specs=(P("replica", "fsdp", None), P("fsdp", None), P("fsdp", None)),
        check_vma=False,
    )
```

time: 137 us -> 114 us (0.83)
  Pallas kernels: 132 us -> 109 us
    pallas_call x1, Pallas kernels: 132 us -> 109 us  [body(): pl.pallas_call(kernel, name='inner_outer', out_shape=(pltpu.VMEM((1, ROWS...]
    unnamed x7 -> x3, local copies, waits for them, and re-layouts: 3.95 us -> 2.64 us
where the time goes in v2:
time: 114 us; the launch traced here: 113 us
  Pallas kernels  109 us (96%)
  local copies, waits for them, and re-layouts  2.64 us (2%)
  between operations  1.29 us (1%)
    pallas_call x1, Pallas kernels, body(): pl.pallas_call(kernel, name='inner_outer', out_shape=(pltpu.VMEM((1, ROWS...  109 us
    unnamed x3, local copies, waits for them, and re-layouts  2.64 us

profile of v2, /device:TPU:2, one launch (start us, length us, event | category | flops | bytes accessed | tf_op | source)
XLA Modules:
  0.0 112.9 jit_solution(17255524855850999374)
XLA Ops:
  1.3 108.9 %inner_outer.1 = (bf16[1,1536,256]{2,1,0:T(8,128)(2,1)S(1)}, f32[1536,128]{1,0:T(8,128)S(1)}, f32[1536,128]{1,0:T(8,128)S(1)}) custom-call(bf16[1,2,128,12288]{3,2,1,0:T(8,128)(2,1)} %x_hbm.1, bf16[1,2,128,256]{3,2,1,0:T(8,128)(2,1)} %cot_hbm.1, bf16[1,1536,256]{2,1,0:T(8,128)(2,1)} %w_hbm.1, f32[1,1536,256]{2,1,0:T(8,128)} %m_hbm.1, f32[1,1536,256]{2,1,0:T(8,128)} %v_hbm.1, ...), custom_call_target="tpu_custom_call" | custom-call | tf_op jit(solution)/shard_map/inner_outer/pallas_call | solution.py:463
  110.2 0.9 copy.15
  111.1 0.9 copy.16
  112.0 0.9 copy.17

commit v3 on v2

--- a/solution.py
+++ b/solution.py
@@ -16,9 +16,35 @@
 FSDP = 8
 ROWS = D // FSDP
 REPLICAS = 32
-GROUPS = ((64, 64), (64, 48, 16))
-SIZES = ((32, 32, 32, 32), (32, 32, 32, 16, 16))
-AHEAD = 64
+GROUPS = ((80, 48), (64, 48, 16))
+STAGED = ((0, 0),)
+ROW = ((0, 1), (0, 3), (0, 2))
+PLAN = (
+    (48, "scatter", 0, 0),
+    (80, "raw", 0, 0),
+    (96, "fold", 0, 0),
+    (112, "layer", 0, 0),
+    (112, "delta", 0, 0),
+    (128, "pass", 0, 0),
+    (128, "raw", 0, 1),
+    (144, "stack", 0, 0),
+    (160, "delta", 0, 1),
+    (160, "grad", 0, 0),
+    (176, "gather", 0, 0),
+    (176, "grad", 0, 1),
+    (192, "raw", 1, 0),
+    (208, "outer", 0, 0),
+    (224, "delta", 1, 0),
+    (240, "raw", 1, 1),
+    (256, "raw", 1, 2),
+    (256, "grad", 1, 0),
+    (256, "delta", 1, 1),
+    (256, "delta", 1, 2),
+    (256, "grad", 1, 1),
+    (256, "grad", 1, 2),
+)
+SIZES = ((16,) * 8, (16,) * 8)
+AHEAD = 48
 UNITS = tuple((s, sum(SIZES[s][:i]), n) for s in range(STEPS) for i, n in enumerate(SIZES[s]))
 EXCH = tuple((s, g) for s in range(STEPS) for g in range(len(GROUPS[s])))
 TILE = 256
@@ -53,10 +79,13 @@
     rsends = dict(zip(EXCH, scratch[count : 2 * count]))
     rrecvs = dict(zip(EXCH, scratch[2 * count : 3 * count]))
     dbufs = dict(zip(EXCH, scratch[3 * count : 4 * count]))
+    split = 4 * count + len(STAGED)
+    zrecvs = dict(zip(STAGED, scratch[4 * count : split]))
+    folds = dict(zip(STAGED, scratch[split : split + len(STAGED)]))
     (
         cot, w_now, m_now, v_now, grad, anchor, mom, frag, layer_in, partial, pieces, total,
-        loc_sem, own_sem, xs, xr, rs, rr, ds, dr, ls, lr, ps, pr, qs, qr, ts, tr, go_sem,
-    ) = scratch[4 * count :]
+        loc_sem, own_sem, xs, xr, rs, rr, ds, dr, ls, lr, ps, pr, qs, qr, ts, tr, zs, zr, go_sem,
+    ) = scratch[split + len(STAGED) :]
     rep = lax.axis_index("replica")
     fs = lax.axis_index("fsdp")
     zl, yy = fs // 4, lax.rem(fs, 4)
@@ -216,6 +245,7 @@
     width_scale = 1.0 / math.sqrt(D)
     token_scale = 1.0 / math.sqrt(TOK * FSDP)
     rcp, dcp = {}, {}
+    mcp, zcp, fcp = {}, {}, {}
 
     def stage_raw(step, g):
         n = GROUPS[step][g]
@@ -224,27 +254,57 @@
             rsends[step, g][...] = jnp.dot(
                 xbufs[step, g][...], w_now[...], preferred_element_type=jnp.float32
             ).astype(jnp.bfloat16)
-            cps = []
-            for i, o in enumerate(PLANE):
-                cps.append(
+            if (step, g) in STAGED:
+                mcp[step, g] = [
                     remote(
-                        rsends[step, g].at[pl.ds(slot(*o) * n, n)],
-                        rrecvs[step, g].at[i],
-                        rs.at[e, i],
-                        rr.at[e, i],
-                        plane_dev(*o),
+                        rsends[step, g].at[pl.ds(4 * n, 4 * n)],
+                        zrecvs[step, g],
+                        zs.at[e],
+                        zr.at[e],
+                        plane_dev(1, 0),
                     )
-                )
-            rcp[step, g] = cps
+                ]
+                return
+            rcp[step, g] = [
+                remote(
+                    rsends[step, g].at[pl.ds(slot(*o) * n, n)],
+                    rrecvs[step, g].at[i],
+                    rs.at[e, i],
+                    rr.at[e, i],
+                    plane_dev(*o),
+                )
+                for i, o in enumerate(PLANE)
+            ]
+
+    def stage_fold(step, g):
+        n = GROUPS[step][g]
+        e = EXCH.index((step, g))
+        with jax.named_scope(f"fold_{step}_{g}"):
+            arrive(mcp[step, g], f"fold_{step}_{g}")
+            folds[step, g][...] = (
+                rsends[step, g][: 4 * n].astype(jnp.float32) + zrecvs[step, g][...].astype(jnp.float32)
+            ).astype(jnp.bfloat16)
+            rcp[step, g] = [
+                remote(
+                    folds[step, g].at[pl.ds(dy * n, n)],
+                    rrecvs[step, g].at[i],
+                    rs.at[e, i],
+                    rr.at[e, i],
+                    plane_dev(0, dy),
+                )
+                for i, (_, dy) in enumerate(ROW)
+            ]
 
     def stage_delta(step, g):
         n = GROUPS[step][g]
         e = EXCH.index((step, g))
+        staged = (step, g) in STAGED
         with jax.named_scope(f"wait_raw_{step}_{g}"):
             arrive(rcp[step, g], f"raw_{step}_{g}")
         with jax.named_scope(f"delta_{step}_{g}"):
-            raw = rsends[step, g][:n].astype(jnp.float32)
-            for i in range(len(PLANE)):
+            mine = folds[step, g] if staged else rsends[step, g]
+            raw = mine[:n].astype(jnp.float32)
+            for i in range(len(rcp[step, g])):
                 raw = raw + rrecvs[step, g][i].astype(jnp.float32)
             raw = raw * width_scale
             up = cot[step, pl.ds(sum(GROUPS[step][:g]), n)].astype(jnp.float32)
@@ -256,18 +316,36 @@
                 inv = lax.rsqrt(jnp.mean(r * r, axis=-1, keepdims=True) + norm_eps)
                 dotp = jnp.mean(p * r, axis=-1, keepdims=True)
                 dbufs[step, g][:n, cols] = (inv * p - r * (inv * inv * inv) * dotp).astype(jnp.bfloat16)
-            cps = []
-            for i, o in enumerate(PLANE):
-                cps.append(
-                    remote(
-                        dbufs[step, g].at[pl.ds(0, n)],
-                        dbufs[step, g].at[pl.ds(back(*o) * n, n)],
-                        ds.at[e, i],
-                        dr.at[e, i],
-                        plane_dev(*o),
-                    )
-                )
+            targets = ((1, 0),) + ROW if staged else PLANE
+            cps = [
+                remote(
+                    dbufs[step, g].at[pl.ds(0, n)],
+                    dbufs[step, g].at[pl.ds(back(*o) * n, n)],
+                    ds.at[e, i],
+                    dr.at[e, i],
+                    plane_dev(*o),
+                )
+                for i, o in enumerate(targets)
+            ]
+            if staged:
+                zcp[step, g], cps = cps[:1], cps[1:]
             dcp[step, g] = cps
+
+    def stage_pass(step, g):
+        n = GROUPS[step][g]
+        e = EXCH.index((step, g))
+        with jax.named_scope(f"pass_{step}_{g}"):
+            arrive(zcp[step, g], f"pass_{step}_{g}")
+            dcp[step, g] = dcp[step, g] + [
+                remote(
+                    dbufs[step, g].at[pl.ds(4 * n, n)],
+                    dbufs[step, g].at[pl.ds((4 + back(0, dy)) * n, n)],
+                    ds.at[e, 4 + i],
+                    dr.at[e, 4 + i],
+                    plane_dev(0, dy),
+                )
+                for i, (_, dy) in enumerate(ROW)
+            ]
 
     def stage_grad(step, g, finish):
         with jax.named_scope(f"wait_delta_{step}_{g}"):
@@ -361,44 +439,41 @@
 
     held = {}
 
-    def first_moments():
-        get_m.wait()
-        get_v.wait()
-
-    def hold(name, value):
-        held[name] = value
-
-    todo = {
-        48: [lambda: hold("scatter", layer_scatter())],
-        64: [lambda: get_cot.wait(), lambda: stage_raw(0, 0)],
-        96: [lambda: stage_delta(0, 0)],
-        112: [lambda: hold("layer", layer_sum(held["scatter"]))],
-        128: [lambda: stage_raw(0, 1), lambda: stage_grad(0, 0, None)],
-        144: [lambda: hold("stack", stack_sum(held["layer"]))],
-        160: [lambda: stage_delta(0, 1)],
-        176: [lambda: hold("gather", layer_gather(held["stack"]))],
-        192: [first_moments, lambda: stage_grad(0, 1, finish_first), lambda: stage_raw(1, 0)],
-        208: [lambda: outer(held["gather"])],
-        224: [lambda: stage_delta(1, 0)],
-        240: [lambda: stage_raw(1, 1)],
-        256: [
-            lambda: stage_raw(1, 2),
-            lambda: stage_grad(1, 0, None),
-            lambda: stage_delta(1, 1),
-            lambda: stage_delta(1, 2),
-            lambda: stage_grad(1, 1, None),
-            lambda: stage_grad(1, 2, finish_last),
-        ],
-    }
+    def act(kind, step, g):
+        if kind == "raw":
+            stage_raw(step, g)
+        elif kind == "fold":
+            stage_fold(step, g)
+        elif kind == "delta":
+            stage_delta(step, g)
+        elif kind == "pass":
+            stage_pass(step, g)
+        elif kind == "grad":
+            final = g == len(GROUPS[step]) - 1
+            if final and step == 0:
+                get_m.wait()
+                get_v.wait()
+            stage_grad(step, g, (finish_first, finish_last)[step] if final else None)
+        elif kind == "scatter":
+            held["sent"] = layer_scatter()
+        elif kind == "layer":
+            held["sent"] = layer_sum(held["sent"])
+        elif kind == "stack":
+            held["sent"] = stack_sum(held["sent"])
+        elif kind == "gather":
+            held["sent"] = layer_gather(held["sent"])
+        elif kind == "outer":
+            outer(held["sent"])
+
     open_layers()
+    get_cot.wait()
     for k in range(len(UNITS)):
         landed(k)
         before = position
         position += UNITS[k][2]
-        for mark in sorted(todo):
+        for mark, *what in PLAN:
             if before < mark <= position:
-                for act in todo[mark]:
-                    act()
+                act(*what)
         top_up()
     with jax.named_scope("write"):
         for cp in sends:
@@ -426,8 +501,9 @@
     sizes = [GROUPS[s][g] for s, g in EXCH]
     scratch = [pltpu.VMEM((FSDP * n, ROWS), bf) for n in sizes]
     scratch += [pltpu.VMEM((FSDP * n, C), bf) for n in sizes]
-    scratch += [pltpu.VMEM((len(PLANE), n, C), bf) for n in sizes]
+    scratch += [pltpu.VMEM((3 if e in STAGED else 7, GROUPS[e[0]][e[1]], C), bf) for e in EXCH]
     scratch += [pltpu.VMEM((FSDP * n, C), bf) for n in sizes]
+    scratch += [pltpu.VMEM((4 * GROUPS[s][g], C), bf) for s, g in STAGED] * 2
     scratch += [
         pltpu.VMEM((STEPS, TOK, C), bf),
         pltpu.VMEM((ROWS, C), bf),
@@ -457,6 +533,8 @@
         dma((3,)),
         dma((7,)),
         dma((7,)),
+        dma((len(EXCH),)),
+        dma((len(EXCH),)),
         pltpu.SemaphoreType.REGULAR,
     ]
     vmem_spec = pl.BlockSpec(memory_space=pltpu.VMEM)
@@ -478,7 +556,16 @@
         layer_input, cotangent, weight, first_moment, second_moment,
         key_gain.reshape(1, HEAD), frag_index, anchor, momentum,
     )
-    return outs
+    outs = [pltpu.with_memory_space_constraint(o, pltpu.VMEM) for o in outs]
+    return pl.pallas_call(
+        flush,
+        name="flush",
+        out_shape=[jax.ShapeDtypeStruct(o.shape, o.dtype) for o in outs],
+        in_specs=[vmem_spec] * 3,
+        out_specs=[any_spec] * 3,
+        scratch_shapes=[dma((3, PARTS))],
+        compiler_params=pltpu.CompilerParams(vmem_limit_bytes=1 << 20),
+    )(*outs)
 
 
 def solution(mesh):

time: 114 us -> 111 us (0.974)
  local copies, waits for them, and re-layouts: 2.64 us -> 0 us
    unnamed x3 -> x0, local copies, waits for them, and re-layouts: 2.64 us -> none
    pallas_call x1, Pallas kernels: 109 us -> 107 us  [body(): pl.pallas_call(kernel, name='inner_outer', out_shape=(pltpu.VMEM((1, ROWS...]
    pallas_call x0 -> x1, Pallas kernels: none -> 1.45 us  [body(): pl.pallas_call(flush, name='flush', out_shape=[jax.ShapeDtypeStruct(o.sha...]
where the time goes in v3:
time: 111 us; the launch traced here: 110 us
  Pallas kernels  109 us (98%)
  between operations  1.29 us (1%)
    pallas_call x1, Pallas kernels, body(): pl.pallas_call(kernel, name='inner_outer', out_shape=(pltpu.VMEM((1, ROWS...  107 us

profile of v3, /device:TPU:2, one launch (start us, length us, event | category | flops | bytes accessed | tf_op | source)
XLA Modules:
  0.0 109.9 jit_solution(10078014094385738175)
XLA Ops:
  1.3 107.2 %inner_outer.1 = (bf16[1,1536,256]{2,1,0:T(8,128)(2,1)S(1)}, f32[1536,128]{1,0:T(8,128)S(1)}, f32[1536,128]{1,0:T(8,128)S(1)}) custom-call(bf16[1,2,128,12288]{3,2,1,0:T(8,128)(2,1)} %x_hbm.1, bf16[1,2,128,256]{3,2,1,0:T(8,128)(2,1)} %cot_hbm.1, bf16[1,1536,256]{2,1,0:T(8,128)(2,1)} %w_hbm.1, f32[1,1536,256]{2,1,0:T(8,128)} %m_hbm.1, f32[1,1536,256]{2,1,0:T(8,128)} %v_hbm.1, ...), custom_call_target="tpu_custom_call" | custom-call | tf_op jit(solution)/shard_map/inner_outer/pallas_call | solution.py:541
  108.5 1.4 %flush.1 = (bf16[1,1536,256]{2,1,0:T(8,128)(2,1)}, f32[1536,128]{1,0:T(8,128)}, f32[1536,128]{1,0:T(8,128)}) custom-call(bf16[1,1536,256]{2,1,0:T(8,128)(2,1)S(1)} %get-tuple-element.6.a_ref, f32[1536,128]{1,0:T(8,128)S(1)} %get-tuple-element.7.b_ref, f32[1536,128]{1,0:T(8,128)S(1)} %get-tuple-element.8.c_ref), custom_call_target="tpu_custom_call" | custom-call | tf_op jit(solution)/shard_map/flush/pallas_call | solution.py:560

commit v4 on v3

--- a/solution.py
+++ b/solution.py
@@ -17,28 +17,30 @@
 ROWS = D // FSDP
 REPLICAS = 32
 GROUPS = ((80, 48), (64, 48, 16))
-STAGED = ((0, 0),)
+STAGED = ()
+YFIRST = ((0, 0),)
+PASSED = ((0, 0),)
 ROW = ((0, 1), (0, 3), (0, 2))
 PLAN = (
     (48, "scatter", 0, 0),
     (80, "raw", 0, 0),
-    (96, "fold", 0, 0),
     (112, "layer", 0, 0),
-    (112, "delta", 0, 0),
-    (128, "pass", 0, 0),
+    (112, "fold", 0, 0),
+    (128, "delta", 0, 0),
     (128, "raw", 0, 1),
     (144, "stack", 0, 0),
+    (160, "pass", 0, 0),
     (160, "delta", 0, 1),
-    (160, "grad", 0, 0),
     (176, "gather", 0, 0),
-    (176, "grad", 0, 1),
+    (176, "grad", 0, 0),
+    (192, "grad", 0, 1),
     (192, "raw", 1, 0),
     (208, "outer", 0, 0),
     (224, "delta", 1, 0),
     (240, "raw", 1, 1),
     (256, "raw", 1, 2),
+    (256, "delta", 1, 1),
     (256, "grad", 1, 0),
-    (256, "delta", 1, 1),
     (256, "delta", 1, 2),
     (256, "grad", 1, 1),
     (256, "grad", 1, 2),
@@ -79,13 +81,14 @@
     rsends = dict(zip(EXCH, scratch[count : 2 * count]))
     rrecvs = dict(zip(EXCH, scratch[2 * count : 3 * count]))
     dbufs = dict(zip(EXCH, scratch[3 * count : 4 * count]))
-    split = 4 * count + len(STAGED)
-    zrecvs = dict(zip(STAGED, scratch[4 * count : split]))
-    folds = dict(zip(STAGED, scratch[split : split + len(STAGED)]))
+    both = STAGED + YFIRST
+    split = 4 * count + len(both)
+    zrecvs = dict(zip(both, scratch[4 * count : split]))
+    folds = dict(zip(both, scratch[split : split + len(both)]))
     (
         cot, w_now, m_now, v_now, grad, anchor, mom, frag, layer_in, partial, pieces, total,
         loc_sem, own_sem, xs, xr, rs, rr, ds, dr, ls, lr, ps, pr, qs, qr, ts, tr, zs, zr, go_sem,
-    ) = scratch[split + len(STAGED) :]
+    ) = scratch[split + len(both) :]
     rep = lax.axis_index("replica")
     fs = lax.axis_index("fsdp")
     zl, yy = fs // 4, lax.rem(fs, 4)
@@ -265,6 +268,19 @@
                     )
                 ]
                 return
+            if (step, g) in YFIRST:
+                mcp[step, g] = [
+                    remote(
+                        rsends[step, g].at[pl.ds((4 * half + dy) * n, n)],
+                        rrecvs[step, g].at[i, pl.ds(half * n, n)],
+                        rs.at[e, 2 * i + half],
+                        rr.at[e, 2 * i + half],
+                        plane_dev(0, dy),
+                    )
+                    for i, (_, dy) in enumerate(ROW)
+                    for half in range(2)
+                ]
+                return
             rcp[step, g] = [
                 remote(
                     rsends[step, g].at[pl.ds(slot(*o) * n, n)],
@@ -281,6 +297,18 @@
         e = EXCH.index((step, g))
         with jax.named_scope(f"fold_{step}_{g}"):
             arrive(mcp[step, g], f"fold_{step}_{g}")
+            if (step, g) in YFIRST:
+                for half in range(2):
+                    total_half = rsends[step, g][4 * half * n : (4 * half + 1) * n].astype(jnp.float32)
+                    for i in range(len(ROW)):
+                        total_half = total_half + rrecvs[step, g][i, half * n : (half + 1) * n].astype(jnp.float32)
+                    folds[step, g][half * n : (half + 1) * n] = total_half.astype(jnp.bfloat16)
+                rcp[step, g] = [
+                    remote(
+                        folds[step, g].at[pl.ds(n, n)], zrecvs[step, g], zs.at[e], zr.at[e], plane_dev(1, 0)
+                    )
+                ]
+                return
             folds[step, g][...] = (
                 rsends[step, g][: 4 * n].astype(jnp.float32) + zrecvs[step, g][...].astype(jnp.float32)
             ).astype(jnp.bfloat16)
@@ -299,13 +327,18 @@
         n = GROUPS[step][g]
         e = EXCH.index((step, g))
         staged = (step, g) in STAGED
+        yfirst = (step, g) in YFIRST
+        passed = (step, g) in PASSED
         with jax.named_scope(f"wait_raw_{step}_{g}"):
             arrive(rcp[step, g], f"raw_{step}_{g}")
         with jax.named_scope(f"delta_{step}_{g}"):
-            mine = folds[step, g] if staged else rsends[step, g]
+            mine = folds[step, g] if staged or yfirst else rsends[step, g]
             raw = mine[:n].astype(jnp.float32)
-            for i in range(len(rcp[step, g])):
-                raw = raw + rrecvs[step, g][i].astype(jnp.float32)
+            if yfirst:
+                raw = raw + zrecvs[step, g][...].astype(jnp.float32)
+            else:
+                for i in range(len(rcp[step, g])):
+                    raw = raw + rrecvs[step, g][i].astype(jnp.float32)
             raw = raw * width_scale
             up = cot[step, pl.ds(sum(GROUPS[step][:g]), n)].astype(jnp.float32)
             gain = gain_ref[...]
@@ -316,7 +349,7 @@
                 inv = lax.rsqrt(jnp.mean(r * r, axis=-1, keepdims=True) + norm_eps)
                 dotp = jnp.mean(p * r, axis=-1, keepdims=True)
                 dbufs[step, g][:n, cols] = (inv * p - r * (inv * inv * inv) * dotp).astype(jnp.bfloat16)
-            targets = ((1, 0),) + ROW if staged else PLANE
+            targets = ((1, 0),) + ROW if passed else PLANE
             cps = [
                 remote(
                     dbufs[step, g].at[pl.ds(0, n)],
@@ -327,7 +360,7 @@
                 )
                 for i, o in enumerate(targets)
             ]
-            if staged:
+            if passed:
                 zcp[step, g], cps = cps[:1], cps[1:]
             dcp[step, g] = cps
 
@@ -501,9 +534,14 @@
     sizes = [GROUPS[s][g] for s, g in EXCH]
     scratch = [pltpu.VMEM((FSDP * n, ROWS), bf) for n in sizes]
     scratch += [pltpu.VMEM((FSDP * n, C), bf) for n in sizes]
-    scratch += [pltpu.VMEM((3 if e in STAGED else 7, GROUPS[e[0]][e[1]], C), bf) for e in EXCH]
+    for e, n in zip(EXCH, sizes):
+        shape = (3, n, C) if e in STAGED else (3, 2 * n, C) if e in YFIRST else (7, n, C)
+        scratch.append(pltpu.VMEM(shape, bf))
     scratch += [pltpu.VMEM((FSDP * n, C), bf) for n in sizes]
-    scratch += [pltpu.VMEM((4 * GROUPS[s][g], C), bf) for s, g in STAGED] * 2
+    scratch += [pltpu.VMEM((4 * GROUPS[s][g], C), bf) for s, g in STAGED]
+    scratch += [pltpu.VMEM((GROUPS[s][g], C), bf) for s, g in YFIRST]
+    scratch += [pltpu.VMEM((4 * GROUPS[s][g], C), bf) for s, g in STAGED]
+    scratch += [pltpu.VMEM((2 * GROUPS[s][g], C), bf) for s, g in YFIRST]
     scratch += [
         pltpu.VMEM((STEPS, TOK, C), bf),
         pltpu.VMEM((ROWS, C), bf),

time: 111 us -> 109 us (0.982)
  Pallas kernels: 109 us -> 107 us
    pallas_call x1, Pallas kernels: 107 us -> 106 us  [body(): pl.pallas_call(kernel, name='inner_outer', out_shape=(pltpu.VMEM((1, ROWS...]
where the time goes in v4:
time: 109 us; the launch traced here: 108 us
  Pallas kernels  107 us (98%)
  between operations  1.29 us (1%)
    pallas_call x1, Pallas kernels, body(): pl.pallas_call(kernel, name='inner_outer', out_shape=(pltpu.VMEM((1, ROWS...  106 us

profile of v4, /device:TPU:2, one launch (start us, length us, event | category | flops | bytes accessed | tf_op | source)
XLA Modules:
  0.0 108.3 jit_solution(1461002366102204540)
XLA Ops:
  1.3 105.6 %inner_outer.1 = (bf16[1,1536,256]{2,1,0:T(8,128)(2,1)S(1)}, f32[1536,128]{1,0:T(8,128)S(1)}, f32[1536,128]{1,0:T(8,128)S(1)}) custom-call(bf16[1,2,128,12288]{3,2,1,0:T(8,128)(2,1)} %x_hbm.1, bf16[1,2,128,256]{3,2,1,0:T(8,128)(2,1)} %cot_hbm.1, bf16[1,1536,256]{2,1,0:T(8,128)(2,1)} %w_hbm.1, f32[1,1536,256]{2,1,0:T(8,128)} %m_hbm.1, f32[1,1536,256]{2,1,0:T(8,128)} %v_hbm.1, ...), custom_call_target="tpu_custom_call" | custom-call | tf_op jit(solution)/shard_map/inner_outer/pallas_call | solution.py:579
  106.9 1.4 %flush.1 = (bf16[1,1536,256]{2,1,0:T(8,128)(2,1)}, f32[1536,128]{1,0:T(8,128)}, f32[1536,128]{1,0:T(8,128)}) custom-call(bf16[1,1536,256]{2,1,0:T(8,128)(2,1)S(1)} %get-tuple-element.6.a_ref, f32[1536,128]{1,0:T(8,128)S(1)} %get-tuple-element.7.b_ref, f32[1536,128]{1,0:T(8,128)S(1)} %get-tuple-element.8.c_ref), custom_call_target="tpu_custom_call" | custom-call | tf_op jit(solution)/shard_map/flush/pallas_call | solution.py:598

commit v5 on v4

--- a/solution.py
+++ b/solution.py
@@ -36,7 +36,7 @@
     (192, "grad", 0, 1),
     (192, "raw", 1, 0),
     (208, "outer", 0, 0),
-    (224, "delta", 1, 0),
+    (240, "delta", 1, 0),
     (240, "raw", 1, 1),
     (256, "raw", 1, 2),
     (256, "delta", 1, 1),
@@ -50,8 +50,7 @@
 UNITS = tuple((s, sum(SIZES[s][:i]), n) for s in range(STEPS) for i, n in enumerate(SIZES[s]))
 EXCH = tuple((s, g) for s in range(STEPS) for g in range(len(GROUPS[s])))
 TILE = 256
-PARTS = 2
-LIMIT = 61 << 20
+LIMIT = 54 << 20
 
 beta_first = 0.9
 beta_second = 0.95
@@ -73,7 +72,7 @@
 
 def kernel(
     x_hbm, cot_hbm, w_hbm, m_hbm, v_hbm, gain_ref, frag_ref, anchor_hbm, mom_hbm,
-    out_w, newmom, newanchor,
+    w_now, m_now, v_now, grad, newmom, newanchor,
     *scratch,
 ):
     count = len(EXCH)
@@ -86,7 +85,7 @@
     zrecvs = dict(zip(both, scratch[4 * count : split]))
     folds = dict(zip(both, scratch[split : split + len(both)]))
     (
-        cot, w_now, m_now, v_now, grad, anchor, mom, frag, layer_in, partial, pieces, total,
+        cot, anchor, mom, frag, layer_in, partial, pieces, total,
         loc_sem, own_sem, xs, xr, rs, rr, ds, dr, ls, lr, ps, pr, qs, qr, ts, tr, zs, zr, go_sem,
     ) = scratch[split + len(both) :]
     rep = lax.axis_index("replica")
@@ -397,29 +396,14 @@
                 else:
                     finish(rows, acc * token_scale)
 
-    def adamw(rows, g):
-        m = beta_first * m_now[rows] + (1.0 - beta_first) * g
-        v = beta_second * v_now[rows] + (1.0 - beta_second) * g * g
-        w = w_now[rows].astype(jnp.float32)
-        w = w - inner_rate * (m / (jnp.sqrt(v) + adam_eps) + decay_rate * w)
-        return w.astype(jnp.bfloat16), m, v
-
     def finish_first(rows, g):
-        w, m, v = adamw(rows, g)
+        w, m, v = adamw(w_now[rows], m_now[rows], v_now[rows], g)
         w_now[rows] = w
         m_now[rows] = m
         v_now[rows] = v
 
     def finish_last(rows, g):
-        w, _, _ = adamw(rows, g)
-        mixed = newanchor[rows]
-        for k in range(KV):
-            cols = slice(k * HEAD, (k + 1) * HEAD)
-            mine = w[:, cols].astype(jnp.float32)
-            chosen = lane_first > 0.5 if k == 0 else lane_first < 0.5
-            out_w[0, rows, cols] = jnp.where(
-                chosen, mix_local * mine + (1.0 - mix_local) * mixed, mine
-            ).astype(jnp.bfloat16)
+        grad[rows] = g
 
     def layer_sum(layer_cps):
         with jax.named_scope("layer_sum"):
@@ -513,16 +497,40 @@
             cp.wait_send()
 
 
-def flush(a_ref, b_ref, c_ref, a_out, b_out, c_out, sems):
-    cps = []
-    n = ROWS // PARTS
-    for k in range(PARTS):
-        part = pl.ds(k * n, n)
-        cps.append(pltpu.make_async_copy(a_ref.at[0, part], a_out.at[0, part], sems.at[0, k]))
-        cps.append(pltpu.make_async_copy(b_ref.at[part], b_out.at[part], sems.at[1, k]))
-        cps.append(pltpu.make_async_copy(c_ref.at[part], c_out.at[part], sems.at[2, k]))
+def adamw(w, m, v, g):
+    m = beta_first * m + (1.0 - beta_first) * g
+    v = beta_second * v + (1.0 - beta_second) * g * g
+    w = w.astype(jnp.float32)
+    w = w - inner_rate * (m / (jnp.sqrt(v) + adam_eps) + decay_rate * w)
+    return w.astype(jnp.bfloat16), m, v
+
+
+def finish(
+    frag_ref, w_ref, m_ref, v_ref, g_ref, mom_ref, anchor_ref,
+    merged_out, mom_out, anchor_out, merged, sems, tile_sems,
+):
+    cps = [
+        pltpu.make_async_copy(mom_ref, mom_out, sems.at[0]),
+        pltpu.make_async_copy(anchor_ref, anchor_out, sems.at[1]),
+    ]
     for cp in cps:
         cp.start()
+    first = lax.rem(frag_ref[0], KV) == 0
+    lane_first = jnp.where(first, jnp.float32(1.0), jnp.float32(0.0))
+    for t in range(ROWS // TILE):
+        rows = pl.ds(t * TILE, TILE)
+        w, _, _ = adamw(w_ref[rows], m_ref[rows], v_ref[rows], g_ref[rows])
+        mixed = anchor_ref[rows]
+        for k in range(KV):
+            cols = slice(k * HEAD, (k + 1) * HEAD)
+            mine = w[:, cols].astype(jnp.float32)
+            chosen = lane_first > 0.5 if k == 0 else lane_first < 0.5
+            merged[rows, cols] = jnp.where(
+                chosen, mix_local * mine + (1.0 - mix_local) * mixed, mine
+            ).astype(jnp.bfloat16)
+        cp = pltpu.make_async_copy(merged.at[rows], merged_out.at[0, rows], tile_sems.at[t])
+        cp.start()
+        cps.append(cp)
     for cp in cps:
         cp.wait()
 
@@ -544,10 +552,6 @@
     scratch += [pltpu.VMEM((2 * GROUPS[s][g], C), bf) for s, g in YFIRST]
     scratch += [
         pltpu.VMEM((STEPS, TOK, C), bf),
-        pltpu.VMEM((ROWS, C), bf),
-        pltpu.VMEM((ROWS, C), f32),
-        pltpu.VMEM((ROWS, C), f32),
-        pltpu.VMEM((ROWS, C), f32),
         pltpu.VMEM((ROWS, HEAD), f32),
         pltpu.VMEM((ROWS, HEAD), f32),
         pltpu.VMEM((ROWS, HEAD), bf),
@@ -580,12 +584,15 @@
         kernel,
         name="inner_outer",
         out_shape=(
-            pltpu.VMEM((1, ROWS, C), bf),
+            pltpu.VMEM((ROWS, C), bf),
+            pltpu.VMEM((ROWS, C), f32),
+            pltpu.VMEM((ROWS, C), f32),
+            pltpu.VMEM((ROWS, C), f32),
             pltpu.VMEM((ROWS, HEAD), f32),
             pltpu.VMEM((ROWS, HEAD), f32),
         ),
         in_specs=[any_spec] * 5 + [vmem_spec, pl.BlockSpec(memory_space=pltpu.SMEM)] + [any_spec] * 2,
-        out_specs=(vmem_spec, vmem_spec, vmem_spec),
+        out_specs=(vmem_spec,) * 6,
         scratch_shapes=scratch,
         compiler_params=pltpu.CompilerParams(
             collective_id=0, has_side_effects=True, vmem_limit_bytes=LIMIT
@@ -596,14 +603,18 @@
     )
     outs = [pltpu.with_memory_space_constraint(o, pltpu.VMEM) for o in outs]
     return pl.pallas_call(
-        flush,
-        name="flush",
-        out_shape=[jax.ShapeDtypeStruct(o.shape, o.dtype) for o in outs],
-        in_specs=[vmem_spec] * 3,
+        finish,
+        name="finish",
+        out_shape=[
+            jax.ShapeDtypeStruct((1, ROWS, C), bf),
+            jax.ShapeDtypeStruct((ROWS, HEAD), f32),
+            jax.ShapeDtypeStruct((ROWS, HEAD), f32),
+        ],
+        in_specs=[pl.BlockSpec(memory_space=pltpu.SMEM)] + [vmem_spec] * 6,
         out_specs=[any_spec] * 3,
-        scratch_shapes=[dma((3, PARTS))],
-        compiler_params=pltpu.CompilerParams(vmem_limit_bytes=1 << 20),
-    )(*outs)
+        scratch_shapes=[pltpu.VMEM((ROWS, C), bf), dma((2,)), dma((ROWS // TILE,))],
+        compiler_params=pltpu.CompilerParams(vmem_limit_bytes=2 << 20),
+    )(frag_index, *outs)
 
 
 def solution(mesh):

time: 109 us -> 108 us (level)
  no operation moved by 1% of the time
where the time goes in v5:
time: 108 us
  Pallas kernels  106 us (98%)
  between operations  1.29 us (1%)
    pallas_call x1, Pallas kernels, body(): pl.pallas_call(kernel, name='inner_outer', out_shape=(pltpu.VMEM((ROWS, C...  104 us
    pallas_call x1, Pallas kernels, body(): pl.pallas_call(finish, name='finish', out_shape=[jax.ShapeDtypeStruct((1,...  2.22 us

profile of v5, /device:TPU:2, one launch (start us, length us, event | category | flops | bytes accessed | tf_op | source)
XLA Modules:
  0.0 107.5 jit_solution(15010337951147356458)
XLA Ops:
  1.3 104.0 %inner_outer.1 = (bf16[1536,256]{1,0:T(8,128)(2,1)S(1)}, f32[1536,256]{1,0:T(8,128)S(1)}, f32[1536,256]{1,0:T(8,128)S(1)}, f32[1536,256]{1,0:T(8,128)S(1)}, f32[...) custom-call(bf16[1,2,128,12288]{3,2,1,0:T(8,128)(2,1)} %x_hbm.1, bf16[1,2,128,256]{3,2,1,0:T(8,128)(2,1)} %cot_hbm.1, ...), custom_call_target="tpu_custom_call" | custom-call | tf_op jit(solution)/shard_map/inner_outer/pallas_call | solution.py:583
  105.3 2.2 %finish.1 = (bf16[1,1536,256]{2,1,0:T(8,128)(2,1)}, f32[1536,128]{1,0:T(8,128)}, f32[1536,128]{1,0:T(8,128)}) custom-call(s32[1]{0:T(128)S(6)} %copy.12.frag_ref, bf16[1536,256]{1,0:T(8,128)(2,1)S(1)} %get-tuple-element.9.w_ref, f32[1536,256]{1,0:T(8,128)S(1)} %get-tuple-element.10.m_ref, f32[1536,256]{1,0:T(8,128)S(1)} %get-tuple-element.11.v_ref, ...), custom_call_target="tpu_custom_call" | custom-call | tf_op jit(solution)/shard_map/finish/pallas_call | solution.py:605

commit v6 on v5

--- a/solution.py
+++ b/solution.py
@@ -16,6 +16,7 @@
 FSDP = 8
 ROWS = D // FSDP
 REPLICAS = 32
+LEADER = 21
 GROUPS = ((80, 48), (64, 48, 16))
 STAGED = ()
 YFIRST = ((0, 0),)
@@ -108,7 +109,7 @@
     def stack_dev(dh):
         return (lax.rem(zh + dh, 4) * 8 + xx * 2 + cc, fs)
 
-    leader = rep == REPLICAS - 1
+    leader = rep == LEADER
     with jax.named_scope("entry"):
         bar = pltpu.get_barrier_semaphore()
         for o in PLANE:
@@ -116,7 +117,7 @@
 
         @pl.when(jnp.logical_not(leader))
         def _():
-            pl.semaphore_signal(bar, inc=1, device_id=(REPLICAS - 1, fs), device_id_type=MESH)
+            pl.semaphore_signal(bar, inc=1, device_id=(LEADER, fs), device_id_type=MESH)
             pl.semaphore_wait(bar, len(PLANE))
 
         @pl.when(leader)
@@ -223,9 +224,9 @@
 
             @pl.when(leader)
             def _():
-                @pl.loop(0, REPLICAS - 1)
+                @pl.loop(1, REPLICAS)
                 def _(r):
-                    pl.semaphore_signal(go_sem, inc=1, device_id=(r, fs), device_id_type=MESH)
+                    pl.semaphore_signal(go_sem, inc=1, device_id=(lax.rem(LEADER + r, REPLICAS), fs), device_id_type=MESH)
 
             get_w.wait()
             frag[...] = jnp.where(

time: 108 us -> 108 us (level)
  no operation moved by 1% of the time
where the time goes in v6:
time: 108 us
  Pallas kernels  106 us (98%)
  between operations  1.29 us (1%)
    pallas_call x1, Pallas kernels, body(): pl.pallas_call(kernel, name='inner_outer', out_shape=(pltpu.VMEM((ROWS, C...  104 us
    pallas_call x1, Pallas kernels, body(): pl.pallas_call(finish, name='finish', out_shape=[jax.ShapeDtypeStruct((1,...  2.22 us

profile of v6, /device:TPU:2, one launch (start us, length us, event | category | flops | bytes accessed | tf_op | source)
XLA Modules:
  0.0 107.5 jit_solution(12666514156106552209)
XLA Ops:
  1.3 104.0 %inner_outer.1 = (bf16[1536,256]{1,0:T(8,128)(2,1)S(1)}, f32[1536,256]{1,0:T(8,128)S(1)}, f32[1536,256]{1,0:T(8,128)S(1)}, f32[1536,256]{1,0:T(8,128)S(1)}, f32[...) custom-call(bf16[1,2,128,12288]{3,2,1,0:T(8,128)(2,1)} %x_hbm.1, bf16[1,2,128,256]{3,2,1,0:T(8,128)(2,1)} %cot_hbm.1, ...), custom_call_target="tpu_custom_call" | custom-call | tf_op jit(solution)/shard_map/inner_outer/pallas_call | solution.py:584
  105.3 2.2 %finish.1 = (bf16[1,1536,256]{2,1,0:T(8,128)(2,1)}, f32[1536,128]{1,0:T(8,128)}, f32[1536,128]{1,0:T(8,128)}) custom-call(s32[1]{0:T(128)S(6)} %copy.12.frag_ref, bf16[1536,256]{1,0:T(8,128)(2,1)S(1)} %get-tuple-element.9.w_ref, f32[1536,256]{1,0:T(8,128)S(1)} %get-tuple-element.10.m_ref, f32[1536,256]{1,0:T(8,128)S(1)} %get-tuple-element.11.v_ref, ...), custom_call_target="tpu_custom_call" | custom-call | tf_op jit(solution)/shard_map/finish/pallas_call | solution.py:606
